TPU v7x, 128 devices: a whole 4x4x4 slice. The times are simulated.
128 devices in a mesh: tm: 4 (over z_hi, core), space: 32 (over z_lo, y, x).
Axes of the slice: x: 4, y: 4, z: 4 (z_hi: 2, z_lo: 2; z = z_hi * 2 + z_lo), core: 2. Of those that a mesh axis runs over, the one named last changes fastest.
Arguments:
- start_states: float32 [4, 2, 384, 256, 256], P('tm', None, 'space'), may hold values from -6 to 6
- velocity: float32 [3, 384, 256, 256], P(None, 'space'), may hold values from -0.1 to 0.1
- site_class: int32 [384, 256, 256], P('space'), may hold values from 0 to 7
- attach_rates: float32 [8], replicated, may hold values from 0.01 to 0.2
- detach_rates: float32 [8], replicated, may hold values from 0.005 to 0.1
Outputs:
- new_states: float32 [4, 2, 384, 256, 256], P('tm', None, 'space')
All inputs are finite; a program needn't handle non-finite values.
Results may differ from a plain program's by a relative error of at most 0.0001.
Values sent between devices are 32-bit elements; how exact they have to be, the bound alone decides.
A program may use at most 192 MiB of HBM per device.

v0:
```python
import jax
import jax.numpy as jnp
from jax import lax
from jax.experimental import pallas as pl
from jax.experimental.pallas import tpu as pltpu
from jax.sharding import PartitionSpec as P

MESH = pl.DeviceIdType.MESH
F32 = jnp.float32
BF16 = jnp.bfloat16

ROWS = 12
SIDE = 256
HALF = SIDE // 2
CROWS = ROWS // 2
PAD = 8
CHUNKS = 4
WIDE = SIDE // CHUNKS
SUB = 32
CSUB = 64
SPREAD = 0.08
LAST = 3


def iota(shape, axis):
    return lax.broadcasted_iota(jnp.int32, shape, axis)


def pair_columns(scale):
    match = (iota((SIDE, HALF), 0) // 2) == iota((SIDE, HALF), 1)
    return jnp.where(match, scale, 0.0).astype(BF16)


def pair_rows(scale):
    match = iota((HALF, SIDE), 0) == (iota((HALF, SIDE), 1) // 2)
    return jnp.where(match, scale, 0.0).astype(BF16)


def split(values):
    high = values.astype(BF16)
    return high, (values - high.astype(F32)).astype(BF16)


def dot(left, right):
    return jnp.dot(left, right, preferred_element_type=F32)


def halve(values, rows_table, columns_table):
    high, low = split(values)
    narrow = dot(high, columns_table) + dot(low, columns_table)
    high, low = split(narrow)
    return dot(rows_table, high) + dot(rows_table, low)


def each(count, body):
    lax.fori_loop(0, count, lambda i, _: (body(i), 0)[1], 0)


def main_kernel(
    start, velocity, site_class, attach_table, detach_table,
    ends, g_out,
    ma, mb, p1, n1, p2, n2, p3, n3, cc, al, be, cls,
    snd, hal, st,
    rs_own, rs_next, d_own, dd, g_in,
    mca, mcb, sc, pc1, nc1, pc2, nc2, pc3, nc3, ccc, alc, bec,
    csnd, chal, cst,
    load_sem, snd_sem, hal_sem, st_snd, st_rcv, fw_snd, fw_rcv,
    rs_sem, d_snd, d_rcv, g_sem, c_snd, c_rcv, cst_snd, cst_rcv,
):
    t = lax.axis_index("tm")
    s = lax.axis_index("space")
    has_up = s < 31
    has_dn = s > 0
    up = {"space": jnp.minimum(s + 1, 31)}
    dn = {"space": jnp.maximum(s - 1, 0)}
    core = t % 2
    sibling = {"tm": t + 1 - 2 * core}

    def remote(src, dst, send, recv, to):
        return pltpu.make_async_remote_copy(
            src_ref=src, dst_ref=dst, send_sem=send, recv_sem=recv,
            device_id=to, device_id_type=MESH,
        )

    barrier = pltpu.get_barrier_semaphore()
    for j in (1, 2, 3):
        pl.semaphore_signal(barrier, inc=1, device_id={"tm": (t + j) % 4}, device_id_type=MESH)

    @pl.when(has_up)
    def _():
        pl.semaphore_signal(barrier, inc=1, device_id=up, device_id_type=MESH)

    @pl.when(has_dn)
    def _():
        pl.semaphore_signal(barrier, inc=1, device_id=dn, device_id_type=MESH)

    def loads(i):
        inner = pl.ds(PAD, SIDE)
        pairs = (
            (velocity.at[0, i], p1.at[i + 1]),
            (velocity.at[1, i], p2.at[i]),
            (velocity.at[2, i], p3.at[i]),
            (site_class.at[i], cls.at[i]),
            (start.at[0, i], ma.at[i + 1, inner]),
            (start.at[1, i], ends.at[1, i]),
        )
        return [pltpu.make_async_copy(a, b, load_sem.at[j, i]) for j, (a, b) in enumerate(pairs)]

    def order(k):
        return jnp.where(k % 2 == 0, k // 2, ROWS - 1 - k // 2)

    def start_loads(k):
        for copy in loads(order(k)):
            copy.start()

    each(ROWS, start_loads)

    blank = jnp.zeros((PAD, SIDE), F32)

    def clear(i):
        for ref in (ma, mb):
            ref[i, pl.ds(0, PAD), :] = blank
            ref[i, pl.ds(PAD + SIDE, PAD), :] = blank

    each(ROWS + 2, clear)

    def clear_rows(c):
        rows = pl.ds(PAD + c * SUB, SUB)
        plain = pl.ds(c * SUB, SUB)
        zero = jnp.zeros((SUB, SIDE), F32)
        one = jnp.ones((SUB, SIDE), F32)
        for ref in (ma, mb):
            ref[0, rows, :] = zero
            ref[ROWS + 1, rows, :] = zero
        p1[0, plain, :] = one
        n1[ROWS + 1, plain, :] = one

        @pl.when(jnp.logical_not(has_dn))
        def _():
            st[0, plain, :] = zero
            for k in range(2):
                for lay in range(2):
                    hal[k, 0, lay, plain, :] = zero

        @pl.when(jnp.logical_not(has_up))
        def _():
            st[1, plain, :] = zero
            for k in range(2):
                for lay in range(2):
                    hal[k, 1, lay, plain, :] = zero

    each(SIDE // SUB, clear_rows)

    rows_table = pair_rows(0.25)
    columns_table = pair_columns(0.5)

    def restrict_pair(read):
        return halve(read(0) + read(1), rows_table, columns_table)

    def restrict_shifted(j):
        pc2[j] = restrict_pair(lambda b: p2[2 * j + b])
        pc3[j] = restrict_pair(lambda b: p3[2 * j + b])

    row8 = iota((SUB, SIDE), 0)
    lane = iota((SUB, SIDE), 1)

    def fine_coefs(i):
        def body(c, before):
            y = pl.multiple_of(c * SUB, SUB)
            rows = pl.ds(y, SUB)
            u1 = p1[i + 1, rows, :]
            u2 = p2[i, rows, :]
            u3 = p3[i, rows, :]
            after = p2[i, pl.ds(pl.multiple_of(jnp.minimum(y + SUB, SIDE - PAD), PAD), PAD), :]
            wide = jnp.concatenate([before, u2, after], axis=0)
            wide_plus = jnp.maximum(wide, 0.0) + SPREAD
            wide_minus = wide_plus - wide
            plus1 = jnp.maximum(u1, 0.0) + SPREAD
            minus1 = plus1 - u1
            plus3 = jnp.maximum(u3, 0.0) + SPREAD
            minus3 = plus3 - u3
            kind = cls[i, rows, :]
            attach = jnp.zeros((SUB, SIDE), F32)
            detach = jnp.zeros((SUB, SIDE), F32)
            for level in range(8):
                here = kind == level
                attach = jnp.where(here, attach_table[level], attach)
                detach = jnp.where(here, detach_table[level], detach)
            total = plus1 + minus1 + wide_plus[PAD:PAD + SUB] + wide_minus[PAD:PAD + SUB] + plus3 + minus3
            p1[i + 1, rows, :] = plus1
            n1[i + 1, rows, :] = minus1
            p2[i, rows, :] = jnp.where(row8 + y == 0, 0.0, wide_plus[PAD - 1:PAD - 1 + SUB])
            n2[i, rows, :] = jnp.where(row8 + y == SIDE - 1, 0.0, wide_minus[PAD + 1:PAD + 1 + SUB])
            p3[i, rows, :] = jnp.where(lane == 0, 0.0, pltpu.roll(plus3, 1, 1))
            n3[i, rows, :] = jnp.where(lane == SIDE - 1, 0.0, pltpu.roll(minus3, SIDE - 1, 1))
            cc[i, rows, :] = (1.0 - total) - attach
            al[i, rows, :] = attach
            be[i, rows, :] = detach
            return u2[SUB - PAD:]

        lax.fori_loop(0, SIDE // SUB, body, jnp.zeros((PAD, SIDE), F32))

    sv = ends.at[1]

    def fine_row(src, i, y):
        rows = pl.ds(y, SUB)
        wide = src[i + 1, pl.ds(y, SUB + 2 * PAD), :]
        mid = wide[PAD:PAD + SUB]
        old = sv[i, rows, :]
        off = be[i, rows, :] * old
        padded = pl.ds(y + PAD, SUB)
        out = cc[i, rows, :] * mid + off
        out = out + (p1[i, rows, :] * src[i, padded, :] + n1[i + 2, rows, :] * src[i + 2, padded, :])
        out = out + (p2[i, rows, :] * wide[PAD - 1:PAD - 1 + SUB] + n2[i, rows, :] * wide[PAD + 1:PAD + 1 + SUB])
        out = out + (p3[i, rows, :] * pltpu.roll(mid, 1, 1) + n3[i, rows, :] * pltpu.roll(mid, SIDE - 1, 1))
        return mid, out, (old - off) + al[i, rows, :] * mid

    def step_rows(src, write, first, count, y0, length):
        subs = length // SUB

        def body(n):
            i = first + n // subs
            y = pl.multiple_of(y0 + (n % subs) * SUB, SUB)
            _, out, held = fine_row(src, i, y)
            write(i, y, out)
            sv[i, pl.ds(y, SUB), :] = held

        each(count * subs, body)

    def write_a(i, y, out):
        ma[i + 1, pl.ds(y + PAD, SUB), :] = out

    def write_b(i, y, out):
        mb[i + 1, pl.ds(y + PAD, SUB), :] = out

    def write_end(i, y, out):
        ends[0, i, pl.ds(y, SUB), :] = out

    def attach_edge(i):
        def body(c):
            rows = pl.ds(pl.multiple_of(c * SUB, SUB), SUB)
            mid = ma[i + 1, pl.ds(pl.multiple_of(c * SUB, SUB) + PAD, SUB), :]
            old = sv[i, rows, :]
            sv[i, rows, :] = (old - be[i, rows, :] * old) + al[i, rows, :] * mid

        each(SIDE // SUB, body)

    def edge_copies(k, c):
        rows = pl.ds(c * WIDE, WIDE)
        out = []
        for way, (to, sends, receives) in enumerate(((up, has_up, has_dn), (dn, has_dn, has_up))):
            for lay in range(2):
                out.append((sends, receives, remote(
                    snd.at[way, lay, rows], hal.at[k, way, lay, rows],
                    snd_sem.at[k, way, lay, c], hal_sem.at[k, way, lay, c], to,
                )))
        return out

    def send_edges(k, c):
        for way, i, coef in ((0, ROWS - 1, p1), (1, 0, n1)):
            def body(n, way=way, i=i, coef=coef):
                y = pl.multiple_of(c * WIDE + n * SUB, SUB)
                rows = pl.ds(y, SUB)
                mid, out, _ = fine_row(ma, i, y)
                mb[i + 1, pl.ds(y + PAD, SUB), :] = out
                factor = coef[i + 1, rows, :]
                snd[way, 0, rows, :] = factor * mid
                snd[way, 1, rows, :] = factor * out

            each(WIDE // SUB, body)
        for sends, _, copy in edge_copies(k, c):
            pl.when(sends)(copy.start)

    def take_edges(k, c):
        for _, receives, copy in edge_copies(k, c):
            pl.when(receives)(copy.wait_recv)

        def body(n):
            y = pl.multiple_of(c * WIDE + n * SUB, SUB)
            rows = pl.ds(y, SUB)
            padded = pl.ds(y + PAD, SUB)
            mb[1, padded, :] = mb[1, padded, :] + hal[k, 0, 0, rows, :]
            mb[ROWS, padded, :] = mb[ROWS, padded, :] + hal[k, 1, 0, rows, :]
            mb[0, padded, :] = hal[k, 0, 1, rows, :] + st[0, rows, :] * snd[1, 0, rows, :]
            mb[ROWS + 1, padded, :] = hal[k, 1, 1, rows, :] + st[1, rows, :] * snd[0, 0, rows, :]

        each(WIDE // SUB, body)

    def edge_step(write, c):
        y0 = c * WIDE
        step_rows(mb, write, 0, 2, y0, WIDE)
        step_rows(mb, write, ROWS - 2, 2, y0, WIDE)

    def wait_edges(k, c):
        for sends, _, copy in edge_copies(k, c):
            pl.when(sends)(copy.wait_send)

    def ready(k):
        for copy in loads(order(k)):
            copy.wait()

    each(4, ready)
    restrict_shifted(0)
    restrict_shifted(CROWS - 1)
    each(4, lambda k: fine_coefs(order(k)))

    pl.semaphore_wait(barrier, 3 + has_up.astype(jnp.int32) + has_dn.astype(jnp.int32))

    own_half = pl.ds(core * HALF, HALF)
    other_half = pl.ds((1 - core) * HALF, HALF)
    st_up = remote(p1.at[ROWS, own_half], st.at[0, own_half], st_snd.at[0], st_rcv.at[0], up)
    st_dn = remote(n1.at[1, own_half], st.at[1, own_half], st_snd.at[1], st_rcv.at[1], dn)
    pl.when(has_up)(st_up.start)
    pl.when(has_dn)(st_dn.start)

    each(CHUNKS, lambda c: send_edges(0, c))

    def later(n):
        j = jnp.where(n % 2 == 0, 1 + n // 2, CROWS - 2 - n // 2)
        for b in range(2):
            for copy in loads(2 * j + b):
                copy.wait()
        restrict_shifted(j)
        for b in range(2):
            fine_coefs(2 * j + b)

    each(CROWS - 2, later)

    inner = pl.ds(PAD, SIDE)

    def restrict_start(j):
        rs_own[0, j] = restrict_pair(lambda b: ma[2 * j + b + 1, inner, :])
        rs_own[1, j] = restrict_pair(lambda b: sv[2 * j + b])

    each(CROWS, restrict_start)

    rs_copy = remote(rs_own, rs_next, rs_sem.at[0], rs_sem.at[1], {"tm": (t + 3) % 4})
    pl.when(t > 0)(rs_copy.start)

    def interior(write):
        attach_edge(0)
        attach_edge(ROWS - 1)
        step_rows(ma, write_b, 1, ROWS - 2, 0, SIDE)
        step_rows(mb, write, 2, ROWS - 4, 0, SIDE)

    interior(write_a)

    fw = [remote(st.at[w, own_half], st.at[w, own_half], fw_snd.at[w], fw_rcv.at[w], sibling) for w in range(2)]
    fr = [remote(st.at[w, other_half], st.at[w, other_half], fw_snd.at[w], fw_rcv.at[w], sibling) for w in range(2)]
    for w, exists, copy in ((0, has_dn, st_up), (1, has_up, st_dn)):
        @pl.when(exists)
        def _(w=w, copy=copy):
            copy.wait_recv()
            fw[w].start()
    for w, exists in ((0, has_dn), (1, has_up)):
        pl.when(exists)(fr[w].wait_recv)

    def between(n):
        pl.when(n < CHUNKS)(lambda: take_edges(0, n))
        pl.when(jnp.logical_and(n >= 1, n <= CHUNKS))(lambda: edge_step(write_a, n - 1))

        @pl.when(n >= 2)
        def _():
            wait_edges(0, n - 2)
            send_edges(1, n - 2)

    each(CHUNKS + 2, between)

    interior(write_end)

    def restrict_static(j):
        pc1[j + 1] = restrict_pair(lambda b: p1[2 * j + b + 1] - n1[2 * j + b + 1])
        alc[j] = 2.0 * restrict_pair(lambda b: al[2 * j + b])
        bec[j] = 2.0 * restrict_pair(lambda b: be[2 * j + b])

    crow = iota((HALF, HALF), 0)
    clane = iota((HALF, HALF), 1)
    coarse_spread = 0.5 * SPREAD

    def coarse_coefs(j):
        u1, u2, u3 = pc1[j + 1], pc2[j], pc3[j]
        plus1 = jnp.maximum(u1, 0.0) + coarse_spread
        minus1 = plus1 - u1
        plus2 = jnp.maximum(u2, 0.0) + coarse_spread
        minus2 = plus2 - u2
        plus3 = jnp.maximum(u3, 0.0) + coarse_spread
        minus3 = plus3 - u3
        ccc[j] = (1.0 - (plus1 + minus1 + plus2 + minus2 + plus3 + minus3)) - alc[j]
        pc1[j + 1] = plus1
        nc1[j + 1] = minus1
        pc2[j] = jnp.where(crow == 0, 0.0, pltpu.roll(plus2, 1, 0))
        nc2[j] = jnp.where(crow == HALF - 1, 0.0, pltpu.roll(minus2, HALF - 1, 0))
        pc3[j] = jnp.where(clane == 0, 0.0, pltpu.roll(plus3, 1, 1))
        nc3[j] = jnp.where(clane == HALF - 1, 0.0, pltpu.roll(minus3, HALF - 1, 1))

    is_last = t == LAST
    cst_up = remote(pc1.at[CROWS], cst.at[0], cst_snd.at[0], cst_rcv.at[0], up)
    cst_dn = remote(nc1.at[1], cst.at[1], cst_snd.at[1], cst_rcv.at[1], dn)

    def d_copies(outer):
        out = []
        for comp in range(2):
            if outer:
                places = ((2 + comp, pl.ds(0, 1)), (4 + comp, pl.ds(CROWS - 1, 1)))
            else:
                places = ((comp, pl.ds(1, CROWS - 2)),)
            for n, rows in places:
                out.append(remote(
                    d_own.at[comp, rows], dd.at[t + 1, comp, rows],
                    d_snd.at[n], d_rcv.at[t, n], {"tm": LAST},
                ))
        return out

    def jump(j):
        for comp in range(2):
            d_own[comp, j] = restrict_pair(lambda b: ends[comp, 2 * j + b]) - rs_next[comp, j]

    @pl.when(jnp.logical_not(is_last))
    def _():
        rs_copy.wait_recv()
        each(CROWS - 2, lambda n: jump(n + 1))
        for copy in d_copies(False):
            copy.start()

    @pl.when(is_last)
    def _():
        def body(j):
            restrict_static(j)
            coarse_coefs(j)

        each(CROWS, body)
        pl.when(has_up)(cst_up.start)
        pl.when(has_dn)(cst_dn.start)
        zero = jnp.zeros((HALF, HALF), F32)
        one = jnp.ones((HALF, HALF), F32)
        pc1[0] = one
        nc1[CROWS + 1] = one
        margin = jnp.zeros((PAD, HALF), F32)
        middle = pl.ds(PAD, HALF)

        def margins(j):
            for ref in (mca, mcb):
                ref[j, pl.ds(0, PAD), :] = margin
                ref[j, pl.ds(PAD + HALF, PAD), :] = margin

        each(CROWS + 2, margins)
        for j in (0, CROWS + 1):
            mca[j, middle, :] = zero

        @pl.when(jnp.logical_not(has_dn))
        def _():
            cst[0] = zero
            for k in range(3):
                for lay in range(2):
                    chal[k, 0, lay] = zero

        @pl.when(jnp.logical_not(has_up))
        def _():
            cst[1] = zero
            for k in range(3):
                for lay in range(2):
                    chal[k, 1, lay] = zero

        def clear_first(j):
            dd[0, 0, j] = zero
            dd[0, 1, j] = zero

        each(CROWS, clear_first)

    def finish(n):
        pl.when(n < CHUNKS)(lambda: take_edges(1, n))
        pl.when(n >= 1)(lambda: edge_step(write_end, n - 1))

    each(CHUNKS + 1, finish)

    @pl.when(jnp.logical_not(is_last))
    def _():
        jump(0)
        jump(CROWS - 1)
        for copy in d_copies(True):
            copy.start()

    def coarse_row(src, j, y):
        rows = pl.ds(y, CSUB)
        wide = src[j + 1, pl.ds(y, CSUB + 2 * PAD), :]
        mid = wide[PAD:PAD + CSUB]
        old = sc[j, rows, :]
        off = bec[j, rows, :] * old
        padded = pl.ds(y + PAD, CSUB)
        out = ccc[j, rows, :] * mid + off
        out = out + (pc1[j, rows, :] * src[j, padded, :] + nc1[j + 2, rows, :] * src[j + 2, padded, :])
        out = out + (pc2[j, rows, :] * wide[PAD - 1:PAD - 1 + CSUB] + nc2[j, rows, :] * wide[PAD + 1:PAD + 1 + CSUB])
        out = out + (pc3[j, rows, :] * pltpu.roll(mid, 1, 1) + nc3[j, rows, :] * pltpu.roll(mid, HALF - 1, 1))
        return mid, out, (old - off) + alc[j, rows, :] * mid

    halves = HALF // CSUB

    def coarse_first(j, with_held):
        for c in range(halves):
            y = c * CSUB
            _, out, held = coarse_row(mca, j, y)
            mcb[j + 1, pl.ds(y + PAD, CSUB), :] = out
            if with_held:
                sc[j, pl.ds(y, CSUB), :] = held

    def coarse_second(turn, j):
        for c in range(halves):
            y = c * CSUB
            _, out, held = coarse_row(mcb, j, y)
            dd[turn, 0, j, pl.ds(y, CSUB), :] = out
            dd[turn, 1, j, pl.ds(y, CSUB), :] = held

    def coarse_edge_copies(turn):
        out = []
        for way, (to, sends, receives) in enumerate(((up, has_up, has_dn), (dn, has_dn, has_up))):
            for lay in range(2):
                out.append((sends, receives, remote(
                    csnd.at[turn - 1, way, lay], chal.at[turn - 1, way, lay],
                    c_snd.at[turn - 1, way, lay], c_rcv.at[turn - 1, way, lay], to,
                )))
        return out

    middle = pl.ds(PAD, HALF)

    def chain(turn):
        for comp in range(2):
            for n, rows in ((comp, pl.ds(1, CROWS - 2)), (2 + comp, pl.ds(0, 1)), (4 + comp, pl.ds(CROWS - 1, 1))):
                remote(
                    d_own.at[comp, rows], dd.at[turn, comp, rows],
                    d_snd.at[n], d_rcv.at[turn - 1, n], {"tm": 0},
                ).wait_recv()

        def gather(j):
            mca[j + 1, middle, :] = dd[turn, 0, j] + dd[turn - 1, 0, j]
            sc[j] = dd[turn, 1, j] + dd[turn - 1, 1, j]

        each(CROWS, gather)
        for way, j, coef in ((0, CROWS - 1, pc1), (1, 0, nc1)):
            coarse_first(j, False)
            factor = coef[j + 1]
            csnd[turn - 1, way, 0] = factor * mca[j + 1, middle, :]
            csnd[turn - 1, way, 1] = factor * mcb[j + 1, middle, :]
        for sends, _, copy in coarse_edge_copies(turn):
            pl.when(sends)(copy.start)

        for j in (0, CROWS - 1):
            old = sc[j]
            sc[j] = (old - bec[j] * old) + alc[j] * mca[j + 1, middle, :]
        each(CROWS - 2, lambda n: coarse_first(n + 1, True))
        each(CROWS - 4, lambda n: coarse_second(turn, n + 2))

        @pl.when(turn == 1)
        def _():
            pl.when(has_dn)(cst_up.wait_recv)
            pl.when(has_up)(cst_dn.wait_recv)

        for _, receives, copy in coarse_edge_copies(turn):
            pl.when(receives)(copy.wait_recv)
        mcb[1, middle, :] = mcb[1, middle, :] + chal[turn - 1, 0, 0]
        mcb[CROWS, middle, :] = mcb[CROWS, middle, :] + chal[turn - 1, 1, 0]
        mcb[0, middle, :] = chal[turn - 1, 0, 1] + cst[0] * csnd[turn - 1, 1, 0]
        mcb[CROWS + 1, middle, :] = chal[turn - 1, 1, 1] + cst[1] * csnd[turn - 1, 0, 0]
        each(2, lambda n: coarse_second(turn, n))
        each(2, lambda n: coarse_second(turn, n + CROWS - 2))

        @pl.when(turn < LAST)
        def _():
            remote(dd.at[turn], g_in, g_sem.at[turn - 1], g_sem.at[2], {"tm": turn}).start()

    @pl.when(is_last)
    def _():
        each(3, lambda n: chain(n + 1))

        def result(j):
            g_out[0, j] = dd[LAST, 0, j]
            g_out[1, j] = dd[LAST, 1, j]

        each(CROWS, result)

        def sent(n):
            remote(dd.at[n + 1], g_in, g_sem.at[n], g_sem.at[2], {"tm": n + 1}).wait_send()
            return None

        each(2, sent)

        def edges_sent(n):
            for sends, _, copy in coarse_edge_copies(n + 1):
                pl.when(sends)(copy.wait_send)

        each(3, edges_sent)
        pl.when(has_up)(cst_up.wait_send)
        pl.when(has_dn)(cst_dn.wait_send)

    @pl.when(jnp.logical_not(is_last))
    def _():
        for copy in d_copies(False) + d_copies(True):
            copy.wait_send()

        @pl.when(t > 0)
        def _():
            remote(dd.at[1], g_in, g_sem.at[0], g_sem.at[2], {"tm": LAST}).wait_recv()

            def result(j):
                g_out[0, j] = g_in[0, j]
                g_out[1, j] = g_in[1, j]

            each(CROWS, result)

        @pl.when(t == 0)
        def _():
            def result(j):
                g_out[0, j] = jnp.zeros((HALF, HALF), F32)
                g_out[1, j] = jnp.zeros((HALF, HALF), F32)

            each(CROWS, result)

    each(CHUNKS, lambda c: wait_edges(1, c))
    pl.when(has_up)(st_up.wait_send)
    pl.when(has_dn)(st_dn.wait_send)
    pl.when(has_dn)(fw[0].wait_send)
    pl.when(has_up)(fw[1].wait_send)
    pl.when(t > 0)(rs_copy.wait_send)


def final_kernel(ends, g, out, buf, sem):
    wide = (iota((HALF, SIDE), 0) == (iota((HALF, SIDE), 1) // 2)).astype(F32).astype(BF16)
    tall = ((iota((SIDE, HALF), 0) // 2) == iota((SIDE, HALF), 1)).astype(F32).astype(BF16)

    def copy(comp, i):
        return pltpu.make_async_copy(buf.at[comp, i], out.at[comp, i], sem.at[comp, i])

    def body(n):
        comp, j = n // CROWS, n % CROWS
        spread = None
        for part in split(g[comp, j]):
            term = dot(tall, dot(part, wide).astype(BF16))
            spread = term if spread is None else spread + term
        for b in range(2):
            buf[comp, 2 * j + b] = ends[comp, 2 * j + b] + spread
            copy(comp, 2 * j + b).start()

    each(2 * CROWS, body)
    each(2 * ROWS, lambda n: copy(n // ROWS, n % ROWS).wait())


def per_device(start_states, velocity, site_class, attach_rates, detach_rates):
    any_ref = pl.BlockSpec(memory_space=pl.ANY)
    smem = pl.BlockSpec(memory_space=pltpu.SMEM)
    vmem = pl.BlockSpec(memory_space=pltpu.VMEM)
    start = start_states.reshape(start_states.shape[1:])
    plane = (SIDE, SIDE)
    cplane = (HALF, HALF)
    coarse = (2, CROWS) + cplane

    def buf(*shape):
        return pltpu.VMEM(shape, F32)

    brick = buf(ROWS, *plane)
    cbrick = buf(CROWS, *cplane)
    dma = pltpu.SemaphoreType.DMA
    ends, g = pl.pallas_call(
        main_kernel,
        out_shape=(pltpu.VMEM((2, ROWS) + plane, F32), pltpu.VMEM(coarse, F32)),
        in_specs=[any_ref, any_ref, any_ref, smem, smem],
        out_specs=(vmem, vmem),
        scratch_shapes=[
            buf(ROWS + 2, SIDE + 2 * PAD, SIDE), buf(ROWS + 2, SIDE + 2 * PAD, SIDE),
            buf(ROWS + 2, *plane), buf(ROWS + 2, *plane), brick, brick, brick, brick, brick, brick, brick,
            pltpu.VMEM((ROWS,) + plane, jnp.int32),
            buf(2, 2, *plane), buf(2, 2, 2, *plane), buf(2, *plane),
            buf(*coarse), buf(*coarse), buf(*coarse), buf(4, *coarse), buf(*coarse),
            buf(CROWS + 2, HALF + 2 * PAD, HALF), buf(CROWS + 2, HALF + 2 * PAD, HALF), cbrick,
            buf(CROWS + 2, *cplane), buf(CROWS + 2, *cplane), cbrick, cbrick, cbrick, cbrick, cbrick, cbrick, cbrick,
            buf(3, 2, 2, *cplane), buf(3, 2, 2, *cplane), buf(2, *cplane),
            dma((6, ROWS)), dma((2, 2, 2, CHUNKS)), dma((2, 2, 2, CHUNKS)), dma((2,)), dma((2,)), dma((2,)), dma((2,)),
            dma((2,)), dma((6,)), dma((3, 6)), dma((3,)), dma((3, 2, 2)), dma((3, 2, 2)), dma((2,)), dma((2,)),
        ],
        compiler_params=pltpu.CompilerParams(
            collective_id=0, has_side_effects=True, vmem_limit_bytes=56 * 1024 * 1024
        ),
    )(start, velocity, site_class, attach_rates, detach_rates)
    out = pl.pallas_call(
        final_kernel,
        out_shape=jax.ShapeDtypeStruct((2, ROWS) + plane, F32),
        in_specs=[vmem, vmem],
        out_specs=any_ref,
        scratch_shapes=[buf(2, ROWS, *plane), dma((2, ROWS))],
        compiler_params=pltpu.CompilerParams(vmem_limit_bytes=40 * 1024 * 1024),
    )(ends, g)
    return out[None]


def solution(mesh):
    in_specs = (
        P("tm", None, "space", None, None),
        P(None, "space", None, None),
        P("space", None, None),
        P(),
        P(),
    )
    return jax.shard_map(
        per_device, mesh=mesh, in_specs=in_specs, out_specs=P("tm", None, "space", None, None), check_vma=False
    )
```

profile of v0, /device:TPU:1, one launch (start us, length us, event | category | flops | bytes accessed | tf_op | source)
XLA Modules:
  0.0 107.8 jit_solution(10474960259315799905)
XLA Ops:
  0.0 102.1 %shard_map.55 = (f32[2,12,256,256]{3,2,1,0:T(8,128)S(1)}, f32[2,6,128,128]{3,2,1,0:T(8,128)S(1)}) custom-call(f32[2,12,256,256]{3,2,1,0:T(8,128)} %bitcast.2, f32[3,12,256,256]{3,2,1,0:T(8,128)} %velocity.1, s32[12,256,256]{2,1,0:T(8,128)} %site_class.1, f32[8]{0:T(128)} %attach_table.1, f32[8]{0:T(128)} %detach_table.1), custom_call_target="tpu_custom_call" | custom-call | tf_op jit(solution)/shard_map/pallas_call | solution.py:661
  102.1 5.7 %shard_map.56 = f32[2,12,256,256]{3,2,1,0:T(8,128)} custom-call(f32[2,12,256,256]{3,2,1,0:T(8,128)S(1)} %get-tuple-element.7.ends, f32[2,6,128,128]{3,2,1,0:T(8,128)S(1)} %get-tuple-element.8.g), custom_call_target="tpu_custom_call" | custom-call | tf_op jit(solution)/shard_map/pallas_call | solution.py:682
where the time goes:
time: 108 us
  Pallas kernels  108 us (100%)
    pallas_call x1, Pallas kernels, per_device(): pl.pallas_call(main_kernel, out_shape=(pltpu.VMEM((2, ROWS) + plane, F32)...  102 us
    pallas_call x1, Pallas kernels, per_device(): pl.pallas_call(final_kernel, out_shape=jax.ShapeDtypeStruct((2, ROWS) + p...  5.74 us

commit v1 on v0

--- a/solution.py
+++ b/solution.py
@@ -17,7 +17,8 @@
 CHUNKS = 4
 WIDE = SIDE // CHUNKS
 SUB = 32
-CSUB = 64
+COEF = 128
+PLANES = 4
 SPREAD = 0.08
 LAST = 3
 
@@ -31,11 +32,6 @@
     return jnp.where(match, scale, 0.0).astype(BF16)
 
 
-def pair_rows(scale):
-    match = iota((HALF, SIDE), 0) == (iota((HALF, SIDE), 1) // 2)
-    return jnp.where(match, scale, 0.0).astype(BF16)
-
-
 def split(values):
     high = values.astype(BF16)
     return high, (values - high.astype(F32)).astype(BF16)
@@ -45,15 +41,8 @@
     return jnp.dot(left, right, preferred_element_type=F32)
 
 
-def halve(values, rows_table, columns_table):
-    high, low = split(values)
-    narrow = dot(high, columns_table) + dot(low, columns_table)
-    high, low = split(narrow)
-    return dot(rows_table, high) + dot(rows_table, low)
-
-
-def each(count, body):
-    lax.fori_loop(0, count, lambda i, _: (body(i), 0)[1], 0)
+def each(count, body, unroll=1):
+    lax.fori_loop(0, count, lambda i, _: (body(i), 0)[1], 0, unroll=unroll)
 
 
 def main_kernel(
@@ -63,7 +52,7 @@
     snd, hal, st,
     rs_own, rs_next, d_own, dd, g_in,
     mca, mcb, sc, pc1, nc1, pc2, nc2, pc3, nc3, ccc, alc, bec,
-    csnd, chal, cst,
+    csnd, chal, cst, tmp,
     load_sem, snd_sem, hal_sem, st_snd, st_rcv, fw_snd, fw_rcv,
     rs_sem, d_snd, d_rcv, g_sem, c_snd, c_rcv, cst_snd, cst_rcv,
 ):
@@ -100,18 +89,24 @@
             (velocity.at[0, i], p1.at[i + 1]),
             (velocity.at[1, i], p2.at[i]),
             (velocity.at[2, i], p3.at[i]),
-            (site_class.at[i], cls.at[i]),
+            (site_class.at[i], cls.at[slot(i)]),
             (start.at[0, i], ma.at[i + 1, inner]),
             (start.at[1, i], ends.at[1, i]),
         )
         return [pltpu.make_async_copy(a, b, load_sem.at[j, i]) for j, (a, b) in enumerate(pairs)]
 
+    def slot(i):
+        return jnp.where(i < CROWS, 2 * i, 2 * (ROWS - 1 - i) + 1) % 8
+
     def order(k):
         return jnp.where(k % 2 == 0, k // 2, ROWS - 1 - k // 2)
 
     def start_loads(k):
-        for copy in loads(order(k)):
-            copy.start()
+        for n, copy in enumerate(loads(order(k))):
+            if n != 3:
+                copy.start()
+            else:
+                pl.when(k < 8)(copy.start)
 
     each(ROWS, start_loads)
 
@@ -151,27 +146,38 @@
 
     each(SIDE // SUB, clear_rows)
 
-    rows_table = pair_rows(0.25)
-    columns_table = pair_columns(0.5)
-
-    def restrict_pair(read):
-        return halve(read(0) + read(1), rows_table, columns_table)
-
-    def restrict_shifted(j):
-        pc2[j] = restrict_pair(lambda b: p2[2 * j + b])
-        pc3[j] = restrict_pair(lambda b: p3[2 * j + b])
-
-    row8 = iota((SUB, SIDE), 0)
-    lane = iota((SUB, SIDE), 1)
+    columns_table = pair_columns(0.125)
+
+    def restrict_pairs(items):
+        for n, (read, _) in enumerate(items):
+            high, low = split(read(0) + read(1))
+            tmp[n] = dot(high, columns_table) + dot(low, columns_table)
+        for n, (_, write) in enumerate(items):
+            write(tmp[n, pl.ds(0, HALF, 2), :] + tmp[n, pl.ds(1, HALF, 2), :])
+
+    def put(ref, *index):
+        def write(value):
+            ref[index] = value
+        return write
+
+    def restrict_shifted(*pairs):
+        items = []
+        for j in pairs:
+            items.append((lambda b, j=j: p2[2 * j + b], put(pc2, j)))
+            items.append((lambda b, j=j: p3[2 * j + b], put(pc3, j)))
+        restrict_pairs(items)
+
+    row8 = iota((COEF, SIDE), 0)
+    lane = iota((COEF, SIDE), 1)
 
     def fine_coefs(i):
         def body(c, before):
-            y = pl.multiple_of(c * SUB, SUB)
-            rows = pl.ds(y, SUB)
+            y = pl.multiple_of(c * COEF, COEF)
+            rows = pl.ds(y, COEF)
             u1 = p1[i + 1, rows, :]
             u2 = p2[i, rows, :]
             u3 = p3[i, rows, :]
-            after = p2[i, pl.ds(pl.multiple_of(jnp.minimum(y + SUB, SIDE - PAD), PAD), PAD), :]
+            after = p2[i, pl.ds(pl.multiple_of(jnp.minimum(y + COEF, SIDE - PAD), PAD), PAD), :]
             wide = jnp.concatenate([before, u2, after], axis=0)
             wide_plus = jnp.maximum(wide, 0.0) + SPREAD
             wide_minus = wide_plus - wide
@@ -179,71 +185,59 @@
             minus1 = plus1 - u1
             plus3 = jnp.maximum(u3, 0.0) + SPREAD
             minus3 = plus3 - u3
-            kind = cls[i, rows, :]
-            attach = jnp.zeros((SUB, SIDE), F32)
-            detach = jnp.zeros((SUB, SIDE), F32)
+            kind = cls[slot(i), rows, :]
+            attach = jnp.zeros((COEF, SIDE), F32)
+            detach = jnp.zeros((COEF, SIDE), F32)
             for level in range(8):
                 here = kind == level
                 attach = jnp.where(here, attach_table[level], attach)
                 detach = jnp.where(here, detach_table[level], detach)
-            total = plus1 + minus1 + wide_plus[PAD:PAD + SUB] + wide_minus[PAD:PAD + SUB] + plus3 + minus3
+            total = plus1 + minus1 + wide_plus[PAD:PAD + COEF] + wide_minus[PAD:PAD + COEF] + plus3 + minus3
             p1[i + 1, rows, :] = plus1
             n1[i + 1, rows, :] = minus1
-            p2[i, rows, :] = jnp.where(row8 + y == 0, 0.0, wide_plus[PAD - 1:PAD - 1 + SUB])
-            n2[i, rows, :] = jnp.where(row8 + y == SIDE - 1, 0.0, wide_minus[PAD + 1:PAD + 1 + SUB])
+            p2[i, rows, :] = jnp.where(row8 + y == 0, 0.0, wide_plus[PAD - 1:PAD - 1 + COEF])
+            n2[i, rows, :] = jnp.where(row8 + y == SIDE - 1, 0.0, wide_minus[PAD + 1:PAD + 1 + COEF])
             p3[i, rows, :] = jnp.where(lane == 0, 0.0, pltpu.roll(plus3, 1, 1))
             n3[i, rows, :] = jnp.where(lane == SIDE - 1, 0.0, pltpu.roll(minus3, SIDE - 1, 1))
             cc[i, rows, :] = (1.0 - total) - attach
             al[i, rows, :] = attach
             be[i, rows, :] = detach
-            return u2[SUB - PAD:]
-
-        lax.fori_loop(0, SIDE // SUB, body, jnp.zeros((PAD, SIDE), F32))
+            return u2[COEF - PAD:]
+
+        lax.fori_loop(0, SIDE // COEF, body, jnp.zeros((PAD, SIDE), F32), unroll=SIDE // COEF)
 
     sv = ends.at[1]
 
-    def fine_row(src, i, y):
-        rows = pl.ds(y, SUB)
-        wide = src[i + 1, pl.ds(y, SUB + 2 * PAD), :]
-        mid = wide[PAD:PAD + SUB]
+    def fine_row(src, i, y, size):
+        rows = pl.ds(y, size)
+        wide = src[i + 1, pl.ds(y, size + 2 * PAD), :]
+        mid = wide[PAD:PAD + size]
         old = sv[i, rows, :]
         off = be[i, rows, :] * old
-        padded = pl.ds(y + PAD, SUB)
+        padded = pl.ds(y + PAD, size)
         out = cc[i, rows, :] * mid + off
         out = out + (p1[i, rows, :] * src[i, padded, :] + n1[i + 2, rows, :] * src[i + 2, padded, :])
-        out = out + (p2[i, rows, :] * wide[PAD - 1:PAD - 1 + SUB] + n2[i, rows, :] * wide[PAD + 1:PAD + 1 + SUB])
+        out = out + (p2[i, rows, :] * wide[PAD - 1:PAD - 1 + size] + n2[i, rows, :] * wide[PAD + 1:PAD + 1 + size])
         out = out + (p3[i, rows, :] * pltpu.roll(mid, 1, 1) + n3[i, rows, :] * pltpu.roll(mid, SIDE - 1, 1))
         return mid, out, (old - off) + al[i, rows, :] * mid
 
-    def step_rows(src, write, first, count, y0, length):
-        subs = length // SUB
-
-        def body(n):
-            i = first + n // subs
-            y = pl.multiple_of(y0 + (n % subs) * SUB, SUB)
-            _, out, held = fine_row(src, i, y)
-            write(i, y, out)
-            sv[i, pl.ds(y, SUB), :] = held
-
-        each(count * subs, body)
-
-    def write_a(i, y, out):
-        ma[i + 1, pl.ds(y + PAD, SUB), :] = out
-
-    def write_b(i, y, out):
-        mb[i + 1, pl.ds(y + PAD, SUB), :] = out
-
-    def write_end(i, y, out):
-        ends[0, i, pl.ds(y, SUB), :] = out
+    def step_row(src, write, i, y, size):
+        _, out, held = fine_row(src, i, y, size)
+        write(i, y, size, out)
+        sv[i, pl.ds(y, size), :] = held
+
+    def write_a(i, y, size, out):
+        ma[i + 1, pl.ds(y + PAD, size), :] = out
+
+    def write_b(i, y, size, out):
+        mb[i + 1, pl.ds(y + PAD, size), :] = out
+
+    def write_end(i, y, size, out):
+        ends[0, i, pl.ds(y, size), :] = out
 
     def attach_edge(i):
-        def body(c):
-            rows = pl.ds(pl.multiple_of(c * SUB, SUB), SUB)
-            mid = ma[i + 1, pl.ds(pl.multiple_of(c * SUB, SUB) + PAD, SUB), :]
-            old = sv[i, rows, :]
-            sv[i, rows, :] = (old - be[i, rows, :] * old) + al[i, rows, :] * mid
-
-        each(SIDE // SUB, body)
+        old = sv[i]
+        sv[i] = (old - be[i] * old) + al[i] * ma[i + 1, pl.ds(PAD, SIDE), :]
 
     def edge_copies(k, c):
         rows = pl.ds(c * WIDE, WIDE)
@@ -257,17 +251,14 @@
         return out
 
     def send_edges(k, c):
+        y = pl.multiple_of(c * WIDE, WIDE)
+        rows = pl.ds(y, WIDE)
         for way, i, coef in ((0, ROWS - 1, p1), (1, 0, n1)):
-            def body(n, way=way, i=i, coef=coef):
-                y = pl.multiple_of(c * WIDE + n * SUB, SUB)
-                rows = pl.ds(y, SUB)
-                mid, out, _ = fine_row(ma, i, y)
-                mb[i + 1, pl.ds(y + PAD, SUB), :] = out
-                factor = coef[i + 1, rows, :]
-                snd[way, 0, rows, :] = factor * mid
-                snd[way, 1, rows, :] = factor * out
-
-            each(WIDE // SUB, body)
+            mid, out, _ = fine_row(ma, i, y, WIDE)
+            mb[i + 1, pl.ds(y + PAD, WIDE), :] = out
+            factor = coef[i + 1, rows, :]
+            snd[way, 0, rows, :] = factor * mid
+            snd[way, 1, rows, :] = factor * out
         for sends, _, copy in edge_copies(k, c):
             pl.when(sends)(copy.start)
 
@@ -275,21 +266,18 @@
         for _, receives, copy in edge_copies(k, c):
             pl.when(receives)(copy.wait_recv)
 
-        def body(n):
-            y = pl.multiple_of(c * WIDE + n * SUB, SUB)
-            rows = pl.ds(y, SUB)
-            padded = pl.ds(y + PAD, SUB)
-            mb[1, padded, :] = mb[1, padded, :] + hal[k, 0, 0, rows, :]
-            mb[ROWS, padded, :] = mb[ROWS, padded, :] + hal[k, 1, 0, rows, :]
-            mb[0, padded, :] = hal[k, 0, 1, rows, :] + st[0, rows, :] * snd[1, 0, rows, :]
-            mb[ROWS + 1, padded, :] = hal[k, 1, 1, rows, :] + st[1, rows, :] * snd[0, 0, rows, :]
-
-        each(WIDE // SUB, body)
+        y = pl.multiple_of(c * WIDE, WIDE)
+        rows = pl.ds(y, WIDE)
+        padded = pl.ds(y + PAD, WIDE)
+        mb[1, padded, :] = mb[1, padded, :] + hal[k, 0, 0, rows, :]
+        mb[ROWS, padded, :] = mb[ROWS, padded, :] + hal[k, 1, 0, rows, :]
+        mb[0, padded, :] = hal[k, 0, 1, rows, :] + st[0, rows, :] * snd[1, 0, rows, :]
+        mb[ROWS + 1, padded, :] = hal[k, 1, 1, rows, :] + st[1, rows, :] * snd[0, 0, rows, :]
 
     def edge_step(write, c):
-        y0 = c * WIDE
-        step_rows(mb, write, 0, 2, y0, WIDE)
-        step_rows(mb, write, ROWS - 2, 2, y0, WIDE)
+        y = pl.multiple_of(c * WIDE, WIDE)
+        for i in (0, ROWS - 1, 1, ROWS - 2):
+            step_row(mb, write, i, y, WIDE)
 
     def wait_edges(k, c):
         for sends, _, copy in edge_copies(k, c):
@@ -300,9 +288,9 @@
             copy.wait()
 
     each(4, ready)
-    restrict_shifted(0)
-    restrict_shifted(CROWS - 1)
+    restrict_shifted(0, CROWS - 1)
     each(4, lambda k: fine_coefs(order(k)))
+    each(4, lambda k: loads(order(k + 8))[3].start())
 
     pl.semaphore_wait(barrier, 3 + has_up.astype(jnp.int32) + has_dn.astype(jnp.int32))
 
@@ -316,23 +304,28 @@
     each(CHUNKS, lambda c: send_edges(0, c))
 
     def later(n):
-        j = jnp.where(n % 2 == 0, 1 + n // 2, CROWS - 2 - n // 2)
-        for b in range(2):
-            for copy in loads(2 * j + b):
-                copy.wait()
-        restrict_shifted(j)
-        for b in range(2):
-            fine_coefs(2 * j + b)
-
-    each(CROWS - 2, later)
+        pairs = (n + 1, CROWS - 2 - n)
+        for j in pairs:
+            for b in range(2):
+                for copy in loads(2 * j + b):
+                    copy.wait()
+        restrict_shifted(*pairs)
+        for j in pairs:
+            for b in range(2):
+                fine_coefs(2 * j + b)
+
+    each(2, later)
 
     inner = pl.ds(PAD, SIDE)
 
-    def restrict_start(j):
-        rs_own[0, j] = restrict_pair(lambda b: ma[2 * j + b + 1, inner, :])
-        rs_own[1, j] = restrict_pair(lambda b: sv[2 * j + b])
-
-    each(CROWS, restrict_start)
+    def restrict_start(n):
+        items = []
+        for j in (2 * n, 2 * n + 1):
+            items.append((lambda b, j=j: ma[2 * j + b + 1, inner, :], put(rs_own, 0, j)))
+            items.append((lambda b, j=j: sv[2 * j + b], put(rs_own, 1, j)))
+        restrict_pairs(items)
+
+    each(CROWS // 2, restrict_start)
 
     rs_copy = remote(rs_own, rs_next, rs_sem.at[0], rs_sem.at[1], {"tm": (t + 3) % 4})
     pl.when(t > 0)(rs_copy.start)
@@ -340,8 +333,8 @@
     def interior(write):
         attach_edge(0)
         attach_edge(ROWS - 1)
-        step_rows(ma, write_b, 1, ROWS - 2, 0, SIDE)
-        step_rows(mb, write, 2, ROWS - 4, 0, SIDE)
+        each(ROWS - 2, lambda n: step_row(ma, write_b, n + 1, 0, SIDE), unroll=2)
+        each(ROWS - 4, lambda n: step_row(mb, write, n + 2, 0, SIDE), unroll=2)
 
     interior(write_a)
 
@@ -369,9 +362,11 @@
     interior(write_end)
 
     def restrict_static(j):
-        pc1[j + 1] = restrict_pair(lambda b: p1[2 * j + b + 1] - n1[2 * j + b + 1])
-        alc[j] = 2.0 * restrict_pair(lambda b: al[2 * j + b])
-        bec[j] = 2.0 * restrict_pair(lambda b: be[2 * j + b])
+        restrict_pairs((
+            (lambda b: p1[2 * j + b + 1] - n1[2 * j + b + 1], put(pc1, j + 1)),
+            (lambda b: 2.0 * al[2 * j + b], put(alc, j)),
+            (lambda b: 2.0 * be[2 * j + b], put(bec, j)),
+        ))
 
     crow = iota((HALF, HALF), 0)
     clane = iota((HALF, HALF), 1)
@@ -411,14 +406,18 @@
                 ))
         return out
 
-    def jump(j):
-        for comp in range(2):
-            d_own[comp, j] = restrict_pair(lambda b: ends[comp, 2 * j + b]) - rs_next[comp, j]
+    def jump(*rows):
+        def item(comp, j):
+            def write(value):
+                d_own[comp, j] = value - rs_next[comp, j]
+            return lambda b: ends[comp, 2 * j + b], write
+
+        restrict_pairs([item(comp, j) for j in rows for comp in range(2)])
 
     @pl.when(jnp.logical_not(is_last))
     def _():
         rs_copy.wait_recv()
-        each(CROWS - 2, lambda n: jump(n + 1))
+        each(2, lambda n: jump(2 * n + 1, 2 * n + 2))
         for copy in d_copies(False):
             copy.start()
 
@@ -475,52 +474,38 @@
 
     @pl.when(jnp.logical_not(is_last))
     def _():
-        jump(0)
-        jump(CROWS - 1)
+        jump(0, CROWS - 1)
         for copy in d_copies(True):
             copy.start()
 
-    def coarse_row(src, j, y):
-        rows = pl.ds(y, CSUB)
-        wide = src[j + 1, pl.ds(y, CSUB + 2 * PAD), :]
-        mid = wide[PAD:PAD + CSUB]
-        old = sc[j, rows, :]
-        off = bec[j, rows, :] * old
-        padded = pl.ds(y + PAD, CSUB)
-        out = ccc[j, rows, :] * mid + off
-        out = out + (pc1[j, rows, :] * src[j, padded, :] + nc1[j + 2, rows, :] * src[j + 2, padded, :])
-        out = out + (pc2[j, rows, :] * wide[PAD - 1:PAD - 1 + CSUB] + nc2[j, rows, :] * wide[PAD + 1:PAD + 1 + CSUB])
-        out = out + (pc3[j, rows, :] * pltpu.roll(mid, 1, 1) + nc3[j, rows, :] * pltpu.roll(mid, HALF - 1, 1))
-        return mid, out, (old - off) + alc[j, rows, :] * mid
-
-    halves = HALF // CSUB
-
-    def coarse_first(j, with_held):
-        for c in range(halves):
-            y = c * CSUB
-            _, out, held = coarse_row(mca, j, y)
-            mcb[j + 1, pl.ds(y + PAD, CSUB), :] = out
-            if with_held:
-                sc[j, pl.ds(y, CSUB), :] = held
-
-    def coarse_second(turn, j):
-        for c in range(halves):
-            y = c * CSUB
-            _, out, held = coarse_row(mcb, j, y)
-            dd[turn, 0, j, pl.ds(y, CSUB), :] = out
-            dd[turn, 1, j, pl.ds(y, CSUB), :] = held
+    middle = pl.ds(PAD, HALF)
+
+    def coarse_row(src, j):
+        wide = src[j + 1]
+        mid = wide[PAD:PAD + HALF]
+        old = sc[j]
+        off = bec[j] * old
+        out = ccc[j] * mid + off
+        out = out + (pc1[j] * src[j, middle, :] + nc1[j + 2] * src[j + 2, middle, :])
+        out = out + (pc2[j] * wide[PAD - 1:PAD - 1 + HALF] + nc2[j] * wide[PAD + 1:PAD + 1 + HALF])
+        out = out + (pc3[j] * pltpu.roll(mid, 1, 1) + nc3[j] * pltpu.roll(mid, HALF - 1, 1))
+        return mid, out, (old - off) + alc[j] * mid
+
+    def coarse_second(turn, *rows):
+        for j in rows:
+            _, out, held = coarse_row(mcb, j)
+            dd[turn, 0, j] = out
+            dd[turn, 1, j] = held
 
     def coarse_edge_copies(turn):
         out = []
         for way, (to, sends, receives) in enumerate(((up, has_up, has_dn), (dn, has_dn, has_up))):
             for lay in range(2):
                 out.append((sends, receives, remote(
-                    csnd.at[turn - 1, way, lay], chal.at[turn - 1, way, lay],
+                    csnd.at[way, lay], chal.at[turn - 1, way, lay],
                     c_snd.at[turn - 1, way, lay], c_rcv.at[turn - 1, way, lay], to,
                 )))
         return out
-
-    middle = pl.ds(PAD, HALF)
 
     def chain(turn):
         for comp in range(2):
@@ -535,19 +520,28 @@
             sc[j] = dd[turn, 1, j] + dd[turn - 1, 1, j]
 
         each(CROWS, gather)
+        @pl.when(turn > 1)
+        def _():
+            for sends, _, copy in coarse_edge_copies(turn - 1):
+                pl.when(sends)(copy.wait_send)
+
         for way, j, coef in ((0, CROWS - 1, pc1), (1, 0, nc1)):
-            coarse_first(j, False)
+            mid, out, _ = coarse_row(mca, j)
+            mcb[j + 1, middle, :] = out
             factor = coef[j + 1]
-            csnd[turn - 1, way, 0] = factor * mca[j + 1, middle, :]
-            csnd[turn - 1, way, 1] = factor * mcb[j + 1, middle, :]
+            csnd[way, 0] = factor * mid
+            csnd[way, 1] = factor * out
         for sends, _, copy in coarse_edge_copies(turn):
             pl.when(sends)(copy.start)
 
         for j in (0, CROWS - 1):
             old = sc[j]
             sc[j] = (old - bec[j] * old) + alc[j] * mca[j + 1, middle, :]
-        each(CROWS - 2, lambda n: coarse_first(n + 1, True))
-        each(CROWS - 4, lambda n: coarse_second(turn, n + 2))
+        for j in range(1, CROWS - 1):
+            _, out, held = coarse_row(mca, j)
+            mcb[j + 1, middle, :] = out
+            sc[j] = held
+        coarse_second(turn, *range(2, CROWS - 2))
 
         @pl.when(turn == 1)
         def _():
@@ -558,10 +552,9 @@
             pl.when(receives)(copy.wait_recv)
         mcb[1, middle, :] = mcb[1, middle, :] + chal[turn - 1, 0, 0]
         mcb[CROWS, middle, :] = mcb[CROWS, middle, :] + chal[turn - 1, 1, 0]
-        mcb[0, middle, :] = chal[turn - 1, 0, 1] + cst[0] * csnd[turn - 1, 1, 0]
-        mcb[CROWS + 1, middle, :] = chal[turn - 1, 1, 1] + cst[1] * csnd[turn - 1, 0, 0]
-        each(2, lambda n: coarse_second(turn, n))
-        each(2, lambda n: coarse_second(turn, n + CROWS - 2))
+        mcb[0, middle, :] = chal[turn - 1, 0, 1] + cst[0] * csnd[1, 0]
+        mcb[CROWS + 1, middle, :] = chal[turn - 1, 1, 1] + cst[1] * csnd[0, 0]
+        coarse_second(turn, 0, CROWS - 1, 1, CROWS - 2)
 
         @pl.when(turn < LAST)
         def _():
@@ -583,11 +576,9 @@
 
         each(2, sent)
 
-        def edges_sent(n):
-            for sends, _, copy in coarse_edge_copies(n + 1):
-                pl.when(sends)(copy.wait_send)
-
-        each(3, edges_sent)
+        for sends, _, copy in coarse_edge_copies(LAST):
+            pl.when(sends)(copy.wait_send)
+
         pl.when(has_up)(cst_up.wait_send)
         pl.when(has_dn)(cst_dn.wait_send)
 
@@ -639,7 +630,7 @@
             buf[comp, 2 * j + b] = ends[comp, 2 * j + b] + spread
             copy(comp, 2 * j + b).start()
 
-    each(2 * CROWS, body)
+    each(2 * CROWS, body, unroll=2)
     each(2 * ROWS, lambda n: copy(n // ROWS, n % ROWS).wait())
 
 
@@ -666,12 +657,12 @@
         scratch_shapes=[
             buf(ROWS + 2, SIDE + 2 * PAD, SIDE), buf(ROWS + 2, SIDE + 2 * PAD, SIDE),
             buf(ROWS + 2, *plane), buf(ROWS + 2, *plane), brick, brick, brick, brick, brick, brick, brick,
-            pltpu.VMEM((ROWS,) + plane, jnp.int32),
+            pltpu.VMEM((8,) + plane, jnp.int32),
             buf(2, 2, *plane), buf(2, 2, 2, *plane), buf(2, *plane),
             buf(*coarse), buf(*coarse), buf(*coarse), buf(4, *coarse), buf(*coarse),
             buf(CROWS + 2, HALF + 2 * PAD, HALF), buf(CROWS + 2, HALF + 2 * PAD, HALF), cbrick,
             buf(CROWS + 2, *cplane), buf(CROWS + 2, *cplane), cbrick, cbrick, cbrick, cbrick, cbrick, cbrick, cbrick,
-            buf(3, 2, 2, *cplane), buf(3, 2, 2, *cplane), buf(2, *cplane),
+            buf(2, 2, *cplane), buf(3, 2, 2, *cplane), buf(2, *cplane), buf(PLANES, SIDE, HALF),
             dma((6, ROWS)), dma((2, 2, 2, CHUNKS)), dma((2, 2, 2, CHUNKS)), dma((2,)), dma((2,)), dma((2,)), dma((2,)),
             dma((2,)), dma((6,)), dma((3, 6)), dma((3,)), dma((3, 2, 2)), dma((3, 2, 2)), dma((2,)), dma((2,)),
         ],

time: 108 us -> 74 us (0.69)
  the two profiles are of different devices: /device:TPU:1 before, /device:TPU:65 now
where the time goes in v1:
time: 74 us; the launch traced here: 73 us
  Pallas kernels  73 us (99%)
    pallas_call x1, Pallas kernels, per_device(): pl.pallas_call(main_kernel, out_shape=(pltpu.VMEM((2, ROWS) + plane, F32)...  68.5 us
    pallas_call x1, Pallas kernels, per_device(): pl.pallas_call(final_kernel, out_shape=jax.ShapeDtypeStruct((2, ROWS) + p...  4.4 us

profile of v1, /device:TPU:65, one launch (start us, length us, event | category | flops | bytes accessed | tf_op | source)
XLA Modules:
  0.0 73.0 jit_solution(1470676906894286375)
XLA Ops:
  0.0 68.5 %shard_map.55 = (f32[2,12,256,256]{3,2,1,0:T(8,128)S(1)}, f32[2,6,128,128]{3,2,1,0:T(8,128)S(1)}) custom-call(f32[2,12,256,256]{3,2,1,0:T(8,128)} %bitcast.2, f32[3,12,256,256]{3,2,1,0:T(8,128)} %velocity.1, s32[12,256,256]{2,1,0:T(8,128)} %site_class.1, f32[8]{0:T(128)} %attach_table.1, f32[8]{0:T(128)} %detach_table.1), custom_call_target="tpu_custom_call" | custom-call | tf_op jit(solution)/shard_map/pallas_call | solution.py:652
  68.6 4.4 %shard_map.56 = f32[2,12,256,256]{3,2,1,0:T(8,128)} custom-call(f32[2,12,256,256]{3,2,1,0:T(8,128)S(1)} %get-tuple-element.7.ends, f32[2,6,128,128]{3,2,1,0:T(8,128)S(1)} %get-tuple-element.8.g), custom_call_target="tpu_custom_call" | custom-call | tf_op jit(solution)/shard_map/pallas_call | solution.py:673

commit v2 on v1

--- a/solution.py
+++ b/solution.py
@@ -14,7 +14,7 @@
 HALF = SIDE // 2
 CROWS = ROWS // 2
 PAD = 8
-CHUNKS = 4
+CHUNKS = 8
 WIDE = SIDE // CHUNKS
 SUB = 32
 COEF = 128
@@ -54,7 +54,7 @@
     mca, mcb, sc, pc1, nc1, pc2, nc2, pc3, nc3, ccc, alc, bec,
     csnd, chal, cst, tmp,
     load_sem, snd_sem, hal_sem, st_snd, st_rcv, fw_snd, fw_rcv,
-    rs_sem, d_snd, d_rcv, g_sem, c_snd, c_rcv, cst_snd, cst_rcv,
+    rs_sem, turn_sem, d_snd, d_rcv, g_sem, c_snd, c_rcv, cst_snd, cst_rcv,
 ):
     t = lax.axis_index("tm")
     s = lax.axis_index("space")
@@ -102,13 +102,10 @@
         return jnp.where(k % 2 == 0, k // 2, ROWS - 1 - k // 2)
 
     def start_loads(k):
-        for n, copy in enumerate(loads(order(k))):
-            if n != 3:
-                copy.start()
-            else:
-                pl.when(k < 8)(copy.start)
-
-    each(ROWS, start_loads)
+        for copy in loads(order(k)):
+            copy.start()
+
+    each(4, start_loads)
 
     blank = jnp.zeros((PAD, SIDE), F32)
 
@@ -286,11 +283,12 @@
     def ready(k):
         for copy in loads(order(k)):
             copy.wait()
+        start_loads(k + 4)
 
     each(4, ready)
     restrict_shifted(0, CROWS - 1)
     each(4, lambda k: fine_coefs(order(k)))
-    each(4, lambda k: loads(order(k + 8))[3].start())
+    each(4, lambda k: start_loads(k + 8))
 
     pl.semaphore_wait(barrier, 3 + has_up.astype(jnp.int32) + has_dn.astype(jnp.int32))
 
@@ -327,16 +325,18 @@
 
     each(CROWS // 2, restrict_start)
 
-    rs_copy = remote(rs_own, rs_next, rs_sem.at[0], rs_sem.at[1], {"tm": (t + 3) % 4})
+    rs_copy = remote(rs_own, rs_next, rs_sem.at[0], rs_sem.at[1], sibling)
     pl.when(t > 0)(rs_copy.start)
 
-    def interior(write):
-        attach_edge(0)
-        attach_edge(ROWS - 1)
-        each(ROWS - 2, lambda n: step_row(ma, write_b, n + 1, 0, SIDE), unroll=2)
-        each(ROWS - 4, lambda n: step_row(mb, write, n + 2, 0, SIDE), unroll=2)
-
-    interior(write_a)
+    @pl.when(t == 1)
+    def _():
+        for comp in range(2):
+            for j in range(CROWS):
+                rs_next[comp, j] = jnp.zeros((HALF, HALF), F32)
+
+    attach_edge(0)
+    attach_edge(ROWS - 1)
+    each(ROWS - 2, lambda n: step_row(ma, write_b, n + 1, 0, SIDE), unroll=2)
 
     fw = [remote(st.at[w, own_half], st.at[w, own_half], fw_snd.at[w], fw_rcv.at[w], sibling) for w in range(2)]
     fr = [remote(st.at[w, other_half], st.at[w, other_half], fw_snd.at[w], fw_rcv.at[w], sibling) for w in range(2)]
@@ -347,19 +347,6 @@
             fw[w].start()
     for w, exists in ((0, has_dn), (1, has_up)):
         pl.when(exists)(fr[w].wait_recv)
-
-    def between(n):
-        pl.when(n < CHUNKS)(lambda: take_edges(0, n))
-        pl.when(jnp.logical_and(n >= 1, n <= CHUNKS))(lambda: edge_step(write_a, n - 1))
-
-        @pl.when(n >= 2)
-        def _():
-            wait_edges(0, n - 2)
-            send_edges(1, n - 2)
-
-    each(CHUNKS + 2, between)
-
-    interior(write_end)
 
     def restrict_static(j):
         restrict_pairs((
@@ -389,45 +376,92 @@
         nc3[j] = jnp.where(clane == HALF - 1, 0.0, pltpu.roll(minus3, HALF - 1, 1))
 
     is_last = t == LAST
+    runs = t % 2 == 1
     cst_up = remote(pc1.at[CROWS], cst.at[0], cst_snd.at[0], cst_rcv.at[0], up)
     cst_dn = remote(nc1.at[1], cst.at[1], cst_snd.at[1], cst_rcv.at[1], dn)
 
-    def d_copies(outer):
-        out = []
-        for comp in range(2):
-            if outer:
-                places = ((2 + comp, pl.ds(0, 1)), (4 + comp, pl.ds(CROWS - 1, 1)))
-            else:
-                places = ((comp, pl.ds(1, CROWS - 2)),)
-            for n, rows in places:
-                out.append(remote(
-                    d_own.at[comp, rows], dd.at[t + 1, comp, rows],
-                    d_snd.at[n], d_rcv.at[t, n], {"tm": LAST},
-                ))
-        return out
+    def d_pieces(group, comp):
+        if group == 0:
+            return ((comp, pl.ds(2, 2)),)
+        first = 2 - group
+        return ((4 * group - 2 + comp, pl.ds(first, 1)), (4 * group + comp, pl.ds(CROWS - 1 - first, 1)))
+
+    def d_copies(*groups, to=LAST):
+        return [
+            remote(
+                d_own.at[comp, rows], dd.at[t, comp, rows],
+                d_snd.at[0 if to == LAST else 1, n], d_rcv.at[t, n], {"tm": to},
+            )
+            for group in groups for comp in range(2) for n, rows in d_pieces(group, comp)
+        ]
+
+    def send_jump(*groups):
+        for copy in d_copies(*groups):
+            copy.start()
+
+        @pl.when(t == 0)
+        def _():
+            for copy in d_copies(*groups, to=1):
+                copy.start()
+
+    keep = jnp.where(t == 1, 0.0, 1.0)
 
     def jump(*rows):
         def item(comp, j):
             def write(value):
-                d_own[comp, j] = value - rs_next[comp, j]
+                d_own[comp, j] = value - keep * rs_next[comp, j]
             return lambda b: ends[comp, 2 * j + b], write
 
         restrict_pairs([item(comp, j) for j in rows for comp in range(2)])
 
+    def fill(n):
+        def two(write, src, first):
+            for b in range(2):
+                step_row(src, write, first + b, 0, SIDE)
+
+        pl.when(n < 4)(lambda: two(write_a, mb, 2 + 2 * n))
+        pl.when(jnp.logical_and(n >= 4, n < 7))(lambda: two(write_b, ma, 3 + 2 * (n - 4)))
+        pl.when(jnp.logical_and(n >= 7, n < 9))(lambda: two(write_end, mb, 4 + 2 * (n - 7)))
+
+        @pl.when(jnp.logical_and(runs, n >= 4))
+        def _():
+            restrict_static(n - 4)
+            coarse_coefs(n - 4)
+
+        @pl.when(jnp.logical_and(jnp.logical_not(is_last), n == 9))
+        def _():
+            pl.when(t != 1)(rs_copy.wait_recv)
+            jump(2, 3)
+            send_jump(0)
+
+    def between(n):
+        pl.when(n < CHUNKS)(lambda: take_edges(0, n))
+        pl.when(jnp.logical_and(n >= 1, n <= CHUNKS))(lambda: edge_step(write_a, n - 1))
+
+        @pl.when(n >= 2)
+        def _():
+            wait_edges(0, n - 2)
+            send_edges(1, n - 2)
+
+        fill(n)
+
+    each(CHUNKS + 2, between)
+
+    attach_edge(0)
+    attach_edge(ROWS - 1)
+    for i in (1, 2, ROWS - 3, ROWS - 2):
+        step_row(ma, write_b, i, 0, SIDE)
+    for i in (2, 3, ROWS - 4, ROWS - 3):
+        step_row(mb, write_end, i, 0, SIDE)
+
     @pl.when(jnp.logical_not(is_last))
     def _():
-        rs_copy.wait_recv()
-        each(2, lambda n: jump(2 * n + 1, 2 * n + 2))
-        for copy in d_copies(False):
-            copy.start()
-
-    @pl.when(is_last)
-    def _():
-        def body(j):
-            restrict_static(j)
-            coarse_coefs(j)
-
-        each(CROWS, body)
+        jump(1, 4)
+
+        pl.when(t != 1)(lambda: send_jump(1))
+
+    @pl.when(runs)
+    def _():
         pl.when(has_up)(cst_up.start)
         pl.when(has_dn)(cst_dn.start)
         zero = jnp.zeros((HALF, HALF), F32)
@@ -460,12 +494,6 @@
                 for lay in range(2):
                     chal[k, 1, lay] = zero
 
-        def clear_first(j):
-            dd[0, 0, j] = zero
-            dd[0, 1, j] = zero
-
-        each(CROWS, clear_first)
-
     def finish(n):
         pl.when(n < CHUNKS)(lambda: take_edges(1, n))
         pl.when(n >= 1)(lambda: edge_step(write_end, n - 1))
@@ -475,8 +503,20 @@
     @pl.when(jnp.logical_not(is_last))
     def _():
         jump(0, CROWS - 1)
-        for copy in d_copies(True):
-            copy.start()
+
+        @pl.when(t == 1)
+        def _():
+            pl.semaphore_wait(turn_sem, 1)
+            for copy in d_copies(1):
+                copy.start()
+
+        send_jump(2)
+
+        @pl.when(t == 0)
+        def _():
+            for copy in d_copies(2):
+                copy.wait_send()
+            pl.semaphore_signal(turn_sem, inc=1, device_id={"tm": 1}, device_id_type=MESH)
 
     middle = pl.ds(PAD, HALF)
 
@@ -494,8 +534,8 @@
     def coarse_second(turn, *rows):
         for j in rows:
             _, out, held = coarse_row(mcb, j)
-            dd[turn, 0, j] = out
-            dd[turn, 1, j] = held
+            dd[turn - 1, 0, j] = out
+            dd[turn - 1, 1, j] = held
 
     def coarse_edge_copies(turn):
         out = []
@@ -507,19 +547,31 @@
                 )))
         return out
 
+    g_copy = remote(dd.at[1], g_in, g_sem.at[0], g_sem.at[1], {"tm": 2})
+
     def chain(turn):
-        for comp in range(2):
-            for n, rows in ((comp, pl.ds(1, CROWS - 2)), (2 + comp, pl.ds(0, 1)), (4 + comp, pl.ds(CROWS - 1, 1))):
+        for group, comp in ((0, 0), (0, 1), (1, 0), (1, 1), (2, 0), (2, 1)):
+            for n, rows in d_pieces(group, comp):
                 remote(
-                    d_own.at[comp, rows], dd.at[turn, comp, rows],
-                    d_snd.at[n], d_rcv.at[turn - 1, n], {"tm": 0},
+                    d_own.at[comp, rows], dd.at[turn - 1, comp, rows],
+                    d_snd.at[0, n], d_rcv.at[turn - 1, n], {"tm": 0},
                 ).wait_recv()
 
-        def gather(j):
-            mca[j + 1, middle, :] = dd[turn, 0, j] + dd[turn - 1, 0, j]
-            sc[j] = dd[turn, 1, j] + dd[turn - 1, 1, j]
-
-        each(CROWS, gather)
+        taken = jnp.where(turn == 2, 1.0, 0.0)
+        pl.when(turn == 2)(rs_copy.wait_recv)
+
+        @pl.when(turn == 1)
+        def _():
+            for j in range(CROWS):
+                mca[j + 1, middle, :] = dd[0, 0, j]
+                sc[j] = dd[0, 1, j]
+
+        @pl.when(turn > 1)
+        def _():
+            for j in range(CROWS):
+                mca[j + 1, middle, :] = (dd[turn - 1, 0, j] - taken * rs_next[0, j]) + dd[turn - 2, 0, j]
+                sc[j] = (dd[turn - 1, 1, j] - taken * rs_next[1, j]) + dd[turn - 2, 1, j]
+
         @pl.when(turn > 1)
         def _():
             for sends, _, copy in coarse_edge_copies(turn - 1):
@@ -556,54 +608,48 @@
         mcb[CROWS + 1, middle, :] = chal[turn - 1, 1, 1] + cst[1] * csnd[0, 0]
         coarse_second(turn, 0, CROWS - 1, 1, CROWS - 2)
 
-        @pl.when(turn < LAST)
-        def _():
-            remote(dd.at[turn], g_in, g_sem.at[turn - 1], g_sem.at[2], {"tm": turn}).start()
-
-    @pl.when(is_last)
-    def _():
-        each(3, lambda n: chain(n + 1))
+        pl.when(turn == 2)(g_copy.start)
+
+    @pl.when(runs)
+    def _():
+        turns = jnp.where(is_last, LAST, 1)
+        each(turns, lambda n: chain(n + 1))
 
         def result(j):
-            g_out[0, j] = dd[LAST, 0, j]
-            g_out[1, j] = dd[LAST, 1, j]
+            g_out[0, j] = dd[turns - 1, 0, j]
+            g_out[1, j] = dd[turns - 1, 1, j]
 
         each(CROWS, result)
-
-        def sent(n):
-            remote(dd.at[n + 1], g_in, g_sem.at[n], g_sem.at[2], {"tm": n + 1}).wait_send()
-            return None
-
-        each(2, sent)
-
-        for sends, _, copy in coarse_edge_copies(LAST):
+        pl.when(is_last)(g_copy.wait_send)
+        for sends, _, copy in coarse_edge_copies(turns):
             pl.when(sends)(copy.wait_send)
-
         pl.when(has_up)(cst_up.wait_send)
         pl.when(has_dn)(cst_dn.wait_send)
 
-    @pl.when(jnp.logical_not(is_last))
-    def _():
-        for copy in d_copies(False) + d_copies(True):
+    @pl.when(t == 2)
+    def _():
+        g_copy.wait_recv()
+
+        def result(j):
+            g_out[0, j] = g_in[0, j]
+            g_out[1, j] = g_in[1, j]
+
+        each(CROWS, result)
+
+    @pl.when(t == 0)
+    def _():
+        def result(j):
+            g_out[0, j] = jnp.zeros((HALF, HALF), F32)
+            g_out[1, j] = jnp.zeros((HALF, HALF), F32)
+
+        each(CROWS, result)
+        for copy in d_copies(0, 1) + d_copies(0, 1, 2, to=1):
             copy.wait_send()
 
-        @pl.when(t > 0)
-        def _():
-            remote(dd.at[1], g_in, g_sem.at[0], g_sem.at[2], {"tm": LAST}).wait_recv()
-
-            def result(j):
-                g_out[0, j] = g_in[0, j]
-                g_out[1, j] = g_in[1, j]
-
-            each(CROWS, result)
-
-        @pl.when(t == 0)
-        def _():
-            def result(j):
-                g_out[0, j] = jnp.zeros((HALF, HALF), F32)
-                g_out[1, j] = jnp.zeros((HALF, HALF), F32)
-
-            each(CROWS, result)
+    @pl.when(jnp.logical_or(t == 1, t == 2))
+    def _():
+        for copy in d_copies(0, 1, 2):
+            copy.wait_send()
 
     each(CHUNKS, lambda c: wait_edges(1, c))
     pl.when(has_up)(st_up.wait_send)
@@ -659,12 +705,12 @@
             buf(ROWS + 2, *plane), buf(ROWS + 2, *plane), brick, brick, brick, brick, brick, brick, brick,
             pltpu.VMEM((8,) + plane, jnp.int32),
             buf(2, 2, *plane), buf(2, 2, 2, *plane), buf(2, *plane),
-            buf(*coarse), buf(*coarse), buf(*coarse), buf(4, *coarse), buf(*coarse),
+            buf(*coarse), buf(*coarse), buf(*coarse), buf(3, *coarse), buf(*coarse),
             buf(CROWS + 2, HALF + 2 * PAD, HALF), buf(CROWS + 2, HALF + 2 * PAD, HALF), cbrick,
             buf(CROWS + 2, *cplane), buf(CROWS + 2, *cplane), cbrick, cbrick, cbrick, cbrick, cbrick, cbrick, cbrick,
             buf(2, 2, *cplane), buf(3, 2, 2, *cplane), buf(2, *cplane), buf(PLANES, SIDE, HALF),
             dma((6, ROWS)), dma((2, 2, 2, CHUNKS)), dma((2, 2, 2, CHUNKS)), dma((2,)), dma((2,)), dma((2,)), dma((2,)),
-            dma((2,)), dma((6,)), dma((3, 6)), dma((3,)), dma((3, 2, 2)), dma((3, 2, 2)), dma((2,)), dma((2,)),
+            dma((2,)), pltpu.SemaphoreType.REGULAR, dma((2, 10)), dma((3, 10)), dma((2,)), dma((3, 2, 2)), dma((3, 2, 2)), dma((2,)), dma((2,)),
         ],
         compiler_params=pltpu.CompilerParams(
             collective_id=0, has_side_effects=True, vmem_limit_bytes=56 * 1024 * 1024

time: 74 us -> 70.7 us (0.955); the launches traced: 73 us -> 70.6 us
  Pallas kernels: 73 us -> 70.6 us
    pallas_call x1, Pallas kernels: 68.5 us -> 66.2 us  [per_device(): pl.pallas_call(main_kernel, out_shape=(pltpu.VMEM((2, ROWS) + plane, F32)...]
where the time goes in v2:
time: 70.7 us; the launch traced here: 70.6 us
  Pallas kernels  70.6 us (100%)
    pallas_call x1, Pallas kernels, per_device(): pl.pallas_call(main_kernel, out_shape=(pltpu.VMEM((2, ROWS) + plane, F32)...  66.2 us
    pallas_call x1, Pallas kernels, per_device(): pl.pallas_call(final_kernel, out_shape=jax.ShapeDtypeStruct((2, ROWS) + p...  4.41 us

profile of v2, /device:TPU:65, one launch (start us, length us, event | category | flops | bytes accessed | tf_op | source)
XLA Modules:
  0.0 70.6 jit_solution(13221588905590073405)
XLA Ops:
  0.0 66.2 %shard_map.55 = (f32[2,12,256,256]{3,2,1,0:T(8,128)S(1)}, f32[2,6,128,128]{3,2,1,0:T(8,128)S(1)}) custom-call(f32[2,12,256,256]{3,2,1,0:T(8,128)} %bitcast.2, f32[3,12,256,256]{3,2,1,0:T(8,128)} %velocity.1, s32[12,256,256]{2,1,0:T(8,128)} %site_class.1, f32[8]{0:T(128)} %attach_table.1, f32[8]{0:T(128)} %detach_table.1), custom_call_target="tpu_custom_call" | custom-call | tf_op jit(solution)/shard_map/pallas_call | solution.py:698
  66.2 4.4 %shard_map.56 = f32[2,12,256,256]{3,2,1,0:T(8,128)} custom-call(f32[2,12,256,256]{3,2,1,0:T(8,128)S(1)} %get-tuple-element.7.ends, f32[2,6,128,128]{3,2,1,0:T(8,128)S(1)} %get-tuple-element.8.g), custom_call_target="tpu_custom_call" | custom-call | tf_op jit(solution)/shard_map/pallas_call | solution.py:719

commit v3 on v2

--- a/solution.py
+++ b/solution.py
@@ -280,15 +280,22 @@
         for sends, _, copy in edge_copies(k, c):
             pl.when(sends)(copy.wait_send)
 
+    def start_kinds(k):
+        i = order(k + 8)
+        pltpu.make_async_copy(site_class.at[i], cls.at[slot(i)], load_sem.at[3, i]).start()
+
     def ready(k):
         for copy in loads(order(k)):
             copy.wait()
         start_loads(k + 4)
+        for n, copy in enumerate(loads(order(k + 8))):
+            if n != 3:
+                copy.start()
 
     each(4, ready)
     restrict_shifted(0, CROWS - 1)
     each(4, lambda k: fine_coefs(order(k)))
-    each(4, lambda k: start_loads(k + 8))
+    each(4, start_kinds)
 
     pl.semaphore_wait(barrier, 3 + has_up.astype(jnp.int32) + has_dn.astype(jnp.int32))
 
@@ -301,18 +308,23 @@
 
     each(CHUNKS, lambda c: send_edges(0, c))
 
-    def later(n):
-        pairs = (n + 1, CROWS - 2 - n)
-        for j in pairs:
-            for b in range(2):
-                for copy in loads(2 * j + b):
-                    copy.wait()
-        restrict_shifted(*pairs)
-        for j in pairs:
-            for b in range(2):
-                fine_coefs(2 * j + b)
-
-    each(2, later)
+    def more_coefs(p):
+        def row(n):
+            return jnp.where(n < 2, 2 * p, 2 * (CROWS - 1 - p) - 2) + n
+
+        def arrived(n):
+            for copy in loads(row(n))[:4]:
+                copy.wait()
+
+        each(4, arrived)
+        restrict_shifted(p, CROWS - 1 - p)
+        each(4, lambda n: fine_coefs(row(n)))
+
+    def state_arrived(k):
+        for copy in loads(order(k + 4))[4:]:
+            copy.wait()
+
+    each(ROWS - 4, state_arrived)
 
     inner = pl.ds(PAD, SIDE)
 
@@ -326,27 +338,24 @@
     each(CROWS // 2, restrict_start)
 
     rs_copy = remote(rs_own, rs_next, rs_sem.at[0], rs_sem.at[1], sibling)
-    pl.when(t > 0)(rs_copy.start)
-
     @pl.when(t == 1)
     def _():
         for comp in range(2):
             for j in range(CROWS):
                 rs_next[comp, j] = jnp.zeros((HALF, HALF), F32)
 
-    attach_edge(0)
-    attach_edge(ROWS - 1)
-    each(ROWS - 2, lambda n: step_row(ma, write_b, n + 1, 0, SIDE), unroll=2)
+    pl.when(t > 0)(rs_copy.start)
 
     fw = [remote(st.at[w, own_half], st.at[w, own_half], fw_snd.at[w], fw_rcv.at[w], sibling) for w in range(2)]
     fr = [remote(st.at[w, other_half], st.at[w, other_half], fw_snd.at[w], fw_rcv.at[w], sibling) for w in range(2)]
-    for w, exists, copy in ((0, has_dn, st_up), (1, has_up, st_dn)):
-        @pl.when(exists)
-        def _(w=w, copy=copy):
-            copy.wait_recv()
-            fw[w].start()
-    for w, exists in ((0, has_dn), (1, has_up)):
-        pl.when(exists)(fr[w].wait_recv)
+    def share_static():
+        for w, exists, copy in ((0, has_dn, st_up), (1, has_up, st_dn)):
+            @pl.when(exists)
+            def _(w=w, copy=copy):
+                copy.wait_recv()
+                fw[w].start()
+        for w, exists in ((0, has_dn), (1, has_up)):
+            pl.when(exists)(fr[w].wait_recv)
 
     def restrict_static(j):
         restrict_pairs((
@@ -414,51 +423,64 @@
 
         restrict_pairs([item(comp, j) for j in rows for comp in range(2)])
 
+    def among(n, *values):
+        found = n == values[0]
+        for value in values[1:]:
+            found = jnp.logical_or(found, n == value)
+        return found
+
     def fill(n):
-        def two(write, src, first):
-            for b in range(2):
-                step_row(src, write, first + b, 0, SIDE)
-
-        pl.when(n < 4)(lambda: two(write_a, mb, 2 + 2 * n))
-        pl.when(jnp.logical_and(n >= 4, n < 7))(lambda: two(write_b, ma, 3 + 2 * (n - 4)))
-        pl.when(jnp.logical_and(n >= 7, n < 9))(lambda: two(write_end, mb, 4 + 2 * (n - 7)))
-
-        @pl.when(jnp.logical_and(runs, n >= 4))
+        outer = among(n, 1, 11)
+        pl.when(among(n, 0, 2))(lambda: more_coefs(jnp.where(n == 0, 1, 2)))
+        pl.when(outer)(lambda: (attach_edge(0), attach_edge(ROWS - 1), None)[2])
+
+        @pl.when(among(n, 1, 3, 6, 11))
+        def _():
+            def body(m):
+                first = jnp.where(outer, 1 + (ROWS - 4) * m, 3 + 2 * m)
+                for b in range(2):
+                    step_row(ma, write_b, first + b, 0, SIDE)
+
+            each(jnp.where(outer, 2, 3), body)
+
+        @pl.when(among(n, 4, 5))
+        def _():
+            each(4, lambda m: step_row(mb, write_a, 4 * n - 14 + m, 0, SIDE), unroll=2)
+
+        @pl.when(among(n, 7, 11))
+        def _():
+            def body(m):
+                first = jnp.where(outer, 2 + (ROWS - 6) * m, 4 + 2 * m)
+                for b in range(2):
+                    step_row(mb, write_end, first + b, 0, SIDE)
+
+            each(2, body)
+
+        @pl.when(jnp.logical_and(runs, jnp.logical_and(n >= 4, n < 10)))
         def _():
             restrict_static(n - 4)
             coarse_coefs(n - 4)
 
-        @pl.when(jnp.logical_and(jnp.logical_not(is_last), n == 9))
-        def _():
-            pl.when(t != 1)(rs_copy.wait_recv)
-            jump(2, 3)
-            send_jump(0)
+        @pl.when(jnp.logical_and(jnp.logical_not(is_last), among(n, 8, 11)))
+        def _():
+            pl.when(jnp.logical_and(n == 8, t != 1))(rs_copy.wait_recv)
+            p = jnp.where(n == 8, 2, 1)
+            jump(p, CROWS - 1 - p)
+            pl.when(jnp.logical_and(n == 8, t != 1))(lambda: send_jump(0))
+            pl.when(jnp.logical_and(n == 11, t != 1))(lambda: send_jump(1))
 
     def between(n):
-        pl.when(n < CHUNKS)(lambda: take_edges(0, n))
-        pl.when(jnp.logical_and(n >= 1, n <= CHUNKS))(lambda: edge_step(write_a, n - 1))
-
-        @pl.when(n >= 2)
-        def _():
-            wait_edges(0, n - 2)
-            send_edges(1, n - 2)
-
         fill(n)
-
-    each(CHUNKS + 2, between)
-
-    attach_edge(0)
-    attach_edge(ROWS - 1)
-    for i in (1, 2, ROWS - 3, ROWS - 2):
-        step_row(ma, write_b, i, 0, SIDE)
-    for i in (2, 3, ROWS - 4, ROWS - 3):
-        step_row(mb, write_end, i, 0, SIDE)
-
-    @pl.when(jnp.logical_not(is_last))
-    def _():
-        jump(1, 4)
-
-        pl.when(t != 1)(lambda: send_jump(1))
+        pl.when(n == 1)(share_static)
+        pl.when(jnp.logical_and(n >= 1, n <= CHUNKS))(lambda: take_edges(0, n - 1))
+        pl.when(jnp.logical_and(n >= 2, n <= CHUNKS + 1))(lambda: edge_step(write_a, n - 2))
+
+        @pl.when(jnp.logical_and(n >= 3, n <= CHUNKS + 2))
+        def _():
+            wait_edges(0, n - 3)
+            send_edges(1, n - 3)
+
+    each(CHUNKS + 4, between)
 
     @pl.when(runs)
     def _():
@@ -507,16 +529,19 @@
         @pl.when(t == 1)
         def _():
             pl.semaphore_wait(turn_sem, 1)
-            for copy in d_copies(1):
+            for copy in d_copies(0, 1):
                 copy.start()
 
         send_jump(2)
 
         @pl.when(t == 0)
         def _():
-            for copy in d_copies(2):
+            first, second, *rest = d_copies(2)
+            first.wait_send()
+            second.wait_send()
+            pl.semaphore_signal(turn_sem, inc=1, device_id={"tm": 1}, device_id_type=MESH)
+            for copy in rest:
                 copy.wait_send()
-            pl.semaphore_signal(turn_sem, inc=1, device_id={"tm": 1}, device_id_type=MESH)
 
     middle = pl.ds(PAD, HALF)
 

time: 70.7 us -> 69.8 us (0.987)
  Pallas kernels: 70.6 us -> 69.7 us
    pallas_call x1, Pallas kernels: 66.2 us -> 65.3 us  [per_device(): pl.pallas_call(main_kernel, out_shape=(pltpu.VMEM((2, ROWS) + plane, F32)...]
where the time goes in v3:
time: 69.8 us; the launch traced here: 69.7 us
  Pallas kernels  69.7 us (100%)
    pallas_call x1, Pallas kernels, per_device(): pl.pallas_call(main_kernel, out_shape=(pltpu.VMEM((2, ROWS) + plane, F32)...  65.3 us
    pallas_call x1, Pallas kernels, per_device(): pl.pallas_call(final_kernel, out_shape=jax.ShapeDtypeStruct((2, ROWS) + p...  4.41 us

profile of v3, /device:TPU:65, one launch (start us, length us, event | category | flops | bytes accessed | tf_op | source)
XLA Modules:
  0.0 69.7 jit_solution(3322149653024383)
XLA Ops:
  0.0 65.3 %shard_map.55 = (f32[2,12,256,256]{3,2,1,0:T(8,128)S(1)}, f32[2,6,128,128]{3,2,1,0:T(8,128)S(1)}) custom-call(f32[2,12,256,256]{3,2,1,0:T(8,128)} %bitcast.2, f32[3,12,256,256]{3,2,1,0:T(8,128)} %velocity.1, s32[12,256,256]{2,1,0:T(8,128)} %site_class.1, f32[8]{0:T(128)} %attach_table.1, f32[8]{0:T(128)} %detach_table.1), custom_call_target="tpu_custom_call" | custom-call | tf_op jit(solution)/shard_map/pallas_call | solution.py:723
  65.3 4.4 %shard_map.56 = f32[2,12,256,256]{3,2,1,0:T(8,128)} custom-call(f32[2,12,256,256]{3,2,1,0:T(8,128)S(1)} %get-tuple-element.7.ends, f32[2,6,128,128]{3,2,1,0:T(8,128)S(1)} %get-tuple-element.8.g), custom_call_target="tpu_custom_call" | custom-call | tf_op jit(solution)/shard_map/pallas_call | solution.py:744

commit v4 on v3

--- a/solution.py
+++ b/solution.py
@@ -701,7 +701,7 @@
             buf[comp, 2 * j + b] = ends[comp, 2 * j + b] + spread
             copy(comp, 2 * j + b).start()
 
-    each(2 * CROWS, body, unroll=2)
+    each(2 * CROWS, body, unroll=4)
     each(2 * ROWS, lambda n: copy(n // ROWS, n % ROWS).wait())
 
 

time: 69.8 us -> 69.2 us (level)
  no operation moved by 1% of the time
where the time goes in v4:
time: 69.2 us; the launch traced here: 69.1 us
  Pallas kernels  69.1 us (100%)
    pallas_call x1, Pallas kernels, per_device(): pl.pallas_call(main_kernel, out_shape=(pltpu.VMEM((2, ROWS) + plane, F32)...  65.3 us
    pallas_call x1, Pallas kernels, per_device(): pl.pallas_call(final_kernel, out_shape=jax.ShapeDtypeStruct((2, ROWS) + p...  3.84 us

profile of v4, /device:TPU:65, one launch (start us, length us, event | category | flops | bytes accessed | tf_op | source)
XLA Modules:
  0.0 69.1 jit_solution(14056480092099795329)
XLA Ops:
  0.0 65.3 %shard_map.55 = (f32[2,12,256,256]{3,2,1,0:T(8,128)S(1)}, f32[2,6,128,128]{3,2,1,0:T(8,128)S(1)}) custom-call(f32[2,12,256,256]{3,2,1,0:T(8,128)} %bitcast.2, f32[3,12,256,256]{3,2,1,0:T(8,128)} %velocity.1, s32[12,256,256]{2,1,0:T(8,128)} %site_class.1, f32[8]{0:T(128)} %attach_table.1, f32[8]{0:T(128)} %detach_table.1), custom_call_target="tpu_custom_call" | custom-call | tf_op jit(solution)/shard_map/pallas_call | solution.py:723
  65.3 3.8 %shard_map.56 = f32[2,12,256,256]{3,2,1,0:T(8,128)} custom-call(f32[2,12,256,256]{3,2,1,0:T(8,128)S(1)} %get-tuple-element.7.ends, f32[2,6,128,128]{3,2,1,0:T(8,128)S(1)} %get-tuple-element.8.g), custom_call_target="tpu_custom_call" | custom-call | tf_op jit(solution)/shard_map/pallas_call | solution.py:744

commit v5 on v4

--- a/solution.py
+++ b/solution.py
@@ -644,7 +644,7 @@
             g_out[0, j] = dd[turns - 1, 0, j]
             g_out[1, j] = dd[turns - 1, 1, j]
 
-        each(CROWS, result)
+        each(CROWS, result, unroll=CROWS)
         pl.when(is_last)(g_copy.wait_send)
         for sends, _, copy in coarse_edge_copies(turns):
             pl.when(sends)(copy.wait_send)
@@ -659,7 +659,7 @@
             g_out[0, j] = g_in[0, j]
             g_out[1, j] = g_in[1, j]
 
-        each(CROWS, result)
+        each(CROWS, result, unroll=CROWS)
 
     @pl.when(t == 0)
     def _():
@@ -667,7 +667,7 @@
             g_out[0, j] = jnp.zeros((HALF, HALF), F32)
             g_out[1, j] = jnp.zeros((HALF, HALF), F32)
 
-        each(CROWS, result)
+        each(CROWS, result, unroll=CROWS)
         for copy in d_copies(0, 1) + d_copies(0, 1, 2, to=1):
             copy.wait_send()
 
@@ -701,7 +701,7 @@
             buf[comp, 2 * j + b] = ends[comp, 2 * j + b] + spread
             copy(comp, 2 * j + b).start()
 
-    each(2 * CROWS, body, unroll=4)
+    each(2 * CROWS, body, unroll=6)
     each(2 * ROWS, lambda n: copy(n // ROWS, n % ROWS).wait())
 
 

time: 69.2 us -> 69 us (level)
  no operation moved by 1% of the time
where the time goes in v5:
time: 69 us; the launch traced here: 68.8 us
  Pallas kernels  68.8 us (100%)
    pallas_call x1, Pallas kernels, per_device(): pl.pallas_call(main_kernel, out_shape=(pltpu.VMEM((2, ROWS) + plane, F32)...  65.2 us
    pallas_call x1, Pallas kernels, per_device(): pl.pallas_call(final_kernel, out_shape=jax.ShapeDtypeStruct((2, ROWS) + p...  3.61 us

profile of v5, /device:TPU:65, one launch (start us, length us, event | category | flops | bytes accessed | tf_op | source)
XLA Modules:
  0.0 68.8 jit_solution(15367461058205532487)
XLA Ops:
  0.0 65.2 %shard_map.55 = (f32[2,12,256,256]{3,2,1,0:T(8,128)S(1)}, f32[2,6,128,128]{3,2,1,0:T(8,128)S(1)}) custom-call(f32[2,12,256,256]{3,2,1,0:T(8,128)} %bitcast.2, f32[3,12,256,256]{3,2,1,0:T(8,128)} %velocity.1, s32[12,256,256]{2,1,0:T(8,128)} %site_class.1, f32[8]{0:T(128)} %attach_table.1, f32[8]{0:T(128)} %detach_table.1), custom_call_target="tpu_custom_call" | custom-call | tf_op jit(solution)/shard_map/pallas_call | solution.py:723
  65.2 3.6 %shard_map.56 = f32[2,12,256,256]{3,2,1,0:T(8,128)} custom-call(f32[2,12,256,256]{3,2,1,0:T(8,128)S(1)} %get-tuple-element.7.ends, f32[2,6,128,128]{3,2,1,0:T(8,128)S(1)} %get-tuple-element.8.g), custom_call_target="tpu_custom_call" | custom-call | tf_op jit(solution)/shard_map/pallas_call | solution.py:744
